TPU v7x, 512 devices: a whole 4x8x8 slice. The times are simulated.
512 devices in a mesh: tp: 16 (over z_lo, y), dp: 32 (over z_hi, x, core).
Axes of the slice: x: 4, y: 8, z: 8 (z_hi: 4, z_lo: 2; z = z_hi * 2 + z_lo), core: 2. Of those that a mesh axis runs over, the one named last changes fastest.
Arguments:
- tokens: bfloat16 [32, 2048, 5120], P('dp', None, 'tp'), may hold values from -6 to 6
- proximal_weight: bfloat16 [5120, 1024], P('tp'), may hold values from -0.078125 to 0.078125
- current_weight: bfloat16 [5120, 1024], P(('tp', 'dp')), may hold values from -0.078125 to 0.078125
- readout: bfloat16 [32, 2048, 1024], P('dp', 'tp'), may hold values from -0.0625 to 0.0625
- advantage: float32 [32, 2048], P('dp', 'tp'), may hold values from -5 to 5
- lengths: int32 [32, 8], P('dp'), may hold values from 1 to 1024, 2048 in all within a row
Outputs:
- grad_input: bfloat16 [32, 2048, 5120], P('dp', 'tp')
Inputs may be any that keep to these rules, and one draw needn't show every extreme that they name: The lengths of each row sum to 2048; in every row the longest is exactly 1024.
All inputs are finite; a program needn't handle non-finite values.
Results may differ from a plain program's by a relative error of at most 0.0049.
Values may be sent and summed in bfloat16 or wider, within the bound.
A program may use at most 128 MiB of HBM per device.

v0:
```python
import jax
import jax.numpy as jnp
from jax import lax
from jax.sharding import PartitionSpec as P

EPS_HIGH = 0.28
LOSS_MULTIPLIER = 64.0


def token_fractions(packed_row_lengths, token_positions, seg_count):
    seq_ends = jnp.cumsum(packed_row_lengths)
    seq_starts = seq_ends - packed_row_lengths
    inside = (token_positions[None, :] >= seq_starts[:, None]) & (
        token_positions[None, :] < seq_ends[:, None]
    )
    seq_share = 1.0 / (seg_count * packed_row_lengths.astype(jnp.float32))
    return jnp.sum(jnp.where(inside, seq_share[:, None], jnp.float32(0.0)), axis=0)


def token_weights(current_score, proximal_score, adv_values, shares, row_len):
    clipped_ratio = jnp.minimum(jnp.exp(current_score - proximal_score), 1.0 + EPS_HIGH)
    return -LOSS_MULTIPLIER * row_len * shares * clipped_ratio * adv_values


def local(tokens, proximal_weight, current_weight, readout, advantage, lengths):
    tok_dev = readout.shape[1]
    row_len = tokens.shape[1]
    tp_index = lax.axis_index("tp")
    own_positions = tp_index * tok_dev + jnp.arange(tok_dev, dtype=jnp.int32)
    packed_row_lengths = lengths[0]
    shares = token_fractions(packed_row_lengths, own_positions, packed_row_lengths.shape[0])
    all_readout = lax.all_gather(readout, "tp", axis=1, tiled=True)[0]
    local_rows = tokens[0]
    proximal_out = jnp.dot(local_rows, proximal_weight, preferred_element_type=jnp.float32)
    proximal_part = jnp.sum(proximal_out * all_readout, axis=1)
    proximal_score = lax.psum_scatter(proximal_part, "tp", scatter_dimension=0, tiled=True)
    own_tokens = lax.all_to_all(tokens, "tp", split_axis=1, concat_axis=2, tiled=True)[0]
    feature_rows = lax.all_gather(current_weight, "dp", axis=0, tiled=True)
    current_out = jnp.dot(
        own_tokens,
        lax.all_gather(feature_rows, "tp", axis=0, tiled=True),
        preferred_element_type=jnp.float32,
    )
    own_readout = readout[0]
    current_score = jnp.sum(current_out * own_readout, axis=1)
    token_importance_weight = token_weights(
        current_score, proximal_score, advantage[0], shares, row_len
    )
    key_grad = (token_importance_weight[:, None] * own_readout).astype(jnp.bfloat16)
    input_grad = lax.dot_general(
        key_grad,
        lax.all_gather(feature_rows, "tp", axis=0, tiled=True),
        (((1,), (1,)), ((), ())),
        preferred_element_type=jnp.float32,
    )
    return input_grad.astype(jnp.bfloat16)[None]


def solution(mesh):
    in_specs = (
        P("dp", None, "tp"),
        P("tp", None),
        P(("tp", "dp"), None),
        P("dp", "tp", None),
        P("dp", "tp"),
        P("dp", None),
    )
    out_specs = P("dp", "tp", None)
    return jax.shard_map(local, mesh=mesh, in_specs=in_specs, out_specs=out_specs, check_vma=False)
```

profile of v0, /device:TPU:1, one launch (start us, length us, event | category | flops | bytes accessed | tf_op | source)
XLA Modules:
  0.0 275.3 jit_solution(10798203548875763486)
XLA Ops:
  6.5 1.9 copy.16
  8.5 0.0 all-gather.4.cloned.1.call-start
  8.5 55.9 %all-gather = bf16[32,10,1024]{2,1,0:T(8,128)(2,1)S(1)} all-gather(bf16[1,10,1024]{2,1,0:T(8,128)(2,1)} %bitcast.43), channel_id=1, replica_groups=mesh['tp'=16,'dp'=32] {'dp'}, dimensions={0}, use_global_device_ids=true | all-gather | bytes 675840 | tf_op jit(solution)/shard_map/all_gather | solution.py:38
  64.4 1.1 reshape.50
  65.5 5.8 %copy.13 = bf16[1,2048,320]{2,0,1:T(2,128)(2,1)} copy(bf16[1,2048,320]{1,2,0:T(8,128)(2,1)S(1)} %copy-done.3) | data formatting | bytes 2621440 | tf_op args[0]
  71.3 0.5 broadcast.23
  71.8 34.4 %reduce = bf16[2048,320]{1,0:T(8,128)(2,1)S(1)} reduce(bf16[2048,1,320]{2,1,0:T(2,128)(2,1)} %bitcast.38, bf16[]{:T(256)} %broadcast.23), dimensions={1}, to_apply=%bitcast.32.reduce_sub_computation | reduce | bytes 2621442
  106.2 2.6 reshape.53
  108.8 7.3 %all-to-all-start = ((bf16[16,2,20480]{2,1,0:T(2,128)(2,1)}), bf16[16,2,20480]{2,1,0:T(2,128)(2,1)S(1)}, u32[]{:S(2)}, u32[]{:S(2)}) async-start(bf16[16,2,20480]{2,1,0:T(2,128)(2,1)} %reshape.53), calls=%async_computation | async-start | bytes 2621440 | tf_op jit(solution)/shard_map/all_to_all | solution.py:37
  116.2 0.2 reduce-window.7
  116.3 1.3 dynamic-slice
  118.3 0.1 select_reduce_fusion
  118.4 40.3 %all-to-all-done = bf16[16,2,20480]{2,1,0:T(2,128)(2,1)S(1)} async-done(((bf16[16,2,20480]{2,1,0:T(2,128)(2,1)}), bf16[16,2,20480]{2,1,0:T(2,128)(2,1)S(1)}, u32[]{:S(2)}, u32[]{:S(2)}) %all-to-all-start) | async-done | bytes 1310752 | tf_op jit(solution)/shard_map/all_to_all | solution.py:37
  158.8 7.1 %reshape.54 = bf16[2048,1,320]{2,1,0:T(2,128)(2,1)} reshape(bf16[16,2,20480]{2,1,0:T(2,128)(2,1)S(1)} %all-to-all-done) | data formatting | bytes 2621440
  165.8 2.2 copy.18
  168.0 1.2 copy.17
  169.3 0.3 copy.15
  169.7 5.1 %fusion = f32[2048]{0:T(1024)S(1)} fusion(bf16[320,1024]{1,0:T(8,128)(2,1)S(1)} %copy-done, bf16[1,2048,1024]{1,2,0:T(8,128)(2,1)} %all-gather.6.cloned.1.call-done, bf16[1,2048,320]{1,2,0:T(8,128)(2,1)} %param.6), kind=kOutput, calls=%fused_computation.1 | convolution fusion | flops 1348466688 | bytes 6168576 | tf_op jit(solution)/shard_map/dot_general | solution.py:34
  174.8 29.7 %all-reduce = f32[2048]{0:T(1024)S(1)} all-reduce(f32[2048]{0:T(1024)S(1)} %fusion), channel_id=2, replica_groups=mesh['tp'=16,'dp'=32] {'tp'}, use_global_device_ids=true, to_apply=%region_4.5.clone | all-reduce | flops 2048 | bytes 16384
  204.5 52.3 %all-gather.4.cloned.1.call-done = bf16[5120,1024]{1,0:T(8,128)(2,1)} async-done(((bf16[320,1024]{1,0:T(8,128)(2,1)}), bf16[5120,1024]{1,0:T(8,128)(2,1)}) %all-gather.4.cloned.1.call-update) | async-done | bytes 10485776 | tf_op jit(solution)/shard_map/all_gather | solution.py:41
  256.8 5.8 %fusion.3 = f32[128]{0:T(128)S(1)} fusion(bf16[128,5120]{0,1:T(8,128)(2,1)S(1)} %bitcast.40, bf16[5120,1024]{1,0:T(8,128)(2,1)} %all-gather.4.cloned.1.call-done, bf16[1,128,1024]{2,1,0:T(8,128)(2,1)S(1)} %copy-done.2), kind=kOutput, calls=%fused_computation.6 | convolution fusion | flops 1342570368 | bytes 12059136 | tf_op jit(solution)/shard_map/dot_general | solution.py:39
  262.6 0.1 bitcast_multiply_fusion
  262.6 1.1 copy-done.1
  263.8 4.7 %fusion.1 = bf16[1,128,5120]{2,1,0:T(8,128)(2,1)} fusion(bf16[5120,1024]{1,0:T(8,128)(2,1)S(1)} %copy-done.1, bf16[1,128,1024]{2,1,0:T(8,128)(2,1)S(1)} %copy-done.2, f32[128]{0:T(128)S(1)} %bitcast_multiply_fusion), kind=kOutput, calls=%fused_computation.3 | convolution fusion | flops 1343225856 | bytes 12059136 | tf_op jit(solution)/shard_map/dot_general | solution.py:50
  (18 shorter events, 0.1 us)
Async XLA Ops:
  6.5 163.1 %copy-start = (bf16[320,1024]{1,0:T(8,128)(2,1)S(1)}, bf16[320,1024]{1,0:T(8,128)(2,1)}, u32[]{:S(2)}) copy-start(bf16[320,1024]{1,0:T(8,128)(2,1)} %param.7) | copy-start | bytes 1966084
  6.5 59.0 %copy-start.3 = (bf16[1,2048,320]{1,2,0:T(8,128)(2,1)S(1)}, bf16[1,2048,320]{1,2,0:T(8,128)(2,1)}, u32[]{:S(2)}) copy-start(bf16[1,2048,320]{1,2,0:T(8,128)(2,1)} %param.6) | copy-start | bytes 3932164
  6.5 163.1 %all-gather.6.cloned.1.call-start = ((), (), s32[]{:S(2)}) async-start(), calls=%async_computation.2 | async-start | bytes 4456448 | tf_op jit(solution)/shard_map/all_gather | solution.py:32
  8.5 248.3 %all-gather.4.cloned.1.call-start = ((), (), s32[]{:S(2)}) async-start(), calls=%async_computation.1 | async-start | bytes 11141120 | tf_op jit(solution)/shard_map/all_gather | solution.py:41
  106.2 10.0 %copy-start.5 = (s32[1,8]{1,0:T(1,128)S(1)}, s32[1,8]{1,0:T(1,128)}, u32[]{:S(2)}) copy-start(s32[1,8]{1,0:T(1,128)} %param.11) | copy-start | bytes 100
  108.8 50.0 %all-to-all-start = ((bf16[16,2,20480]{2,1,0:T(2,128)(2,1)}), bf16[16,2,20480]{2,1,0:T(2,128)(2,1)S(1)}, u32[]{:S(2)}, u32[]{:S(2)}) async-start(bf16[16,2,20480]{2,1,0:T(2,128)(2,1)} %reshape.53), calls=%async_computation | async-start | bytes 2621440 | tf_op jit(solution)/shard_map/all_to_all | solution.py:37
  169.6 87.2 %copy-start.2 = (bf16[1,128,1024]{2,1,0:T(8,128)(2,1)S(1)}, bf16[1,128,1024]{2,1,0:T(8,128)(2,1)}, u32[]{:S(2)}) copy-start(bf16[1,128,1024]{2,1,0:T(8,128)(2,1)} %param.9) | copy-start | bytes 786436
  256.8 5.8 %copy-start.4 = (f32[1,128]{1,0:T(1,128)S(1)}, f32[1,128]{1,0:T(1,128)}, u32[]{:S(2)}) copy-start(f32[1,128]{1,0:T(1,128)} %param.10) | copy-start | bytes 1540
  256.8 7.0 %copy-start.1 = (bf16[5120,1024]{1,0:T(8,128)(2,1)S(1)}, bf16[5120,1024]{1,0:T(8,128)(2,1)}, u32[]{:S(2)}) copy-start(bf16[5120,1024]{1,0:T(8,128)(2,1)} %all-gather.4.cloned.1.call-done) | copy-start | bytes 31457284
Sparse Core Ops, SparseCore 0:
  9.4 87.1 all-gather.5
  98.6 158.1 all-gather.3
where the time goes:
time: 276 us; the launch traced here: 275 us
  waiting for transfers between devices  92.7 us (34%)
  blocking collectives  85.6 us (31%)
  other arithmetic  34.7 us (13%)
  local copies, waits for them, and re-layouts  25.2 us (9%)
  matrix products  15.5 us (6%)
  between operations  14.2 us (5%)
  starting transfers between devices  7.39 us (3%)
    all_gather x1, blocking collectives, local(): feature_rows = lax.all_gather(current_weight, 'dp', axis=0, tiled=True)  55.9 us
    all_gather x1, waiting for transfers between devices, local(): lax.all_gather(feature_rows, 'tp', axis=0, tiled=True)  52.3 us
    all_to_all x1, waiting for transfers between devices, local(): lax.all_to_all(tokens, 'tp', split_axis=1, concat_axis=2, tiled=True)[0]  40.3 us
    unnamed x1, other arithmetic  34.4 us
    unnamed x1, blocking collectives  29.7 us
    unnamed x20, local copies, waits for them, and re-layouts  23.6 us
    all_to_all x1, starting transfers between devices, local(): lax.all_to_all(tokens, 'tp', split_axis=1, concat_axis=2, tiled=True)[0]  7.34 us
    dot_general x1, matrix products, local(): jnp.dot(own_tokens, lax.all_gather(feature_rows, 'tp', axis=0, tiled=True...  5.75 us
  transfers between devices with their start and end apart: 3, of which 2 were waited for; matrix products, arithmetic and copies ran while one was open for 22% of the time, Pallas kernels for 0%

commit v1 on v0

v1 whole, which is shorter than its diff:
```python
import jax
import jax.numpy as jnp
from jax import lax
from jax.experimental import pallas as pl
from jax.experimental.pallas import tpu as pltpu
from jax.sharding import PartitionSpec as P

EPS_HIGH = 0.28
LOSS_MULTIPLIER = 64.0
BF16, F32 = jnp.bfloat16, jnp.float32

NX, NY, NZ, NZH = 4, 8, 8, 4
OWN, FAR = 6, 7
TOK, SEG, COLS, SLICE, OUT = 128, 1024, 1024, 320, 5120
ROWS, PAD = 10, 16


def dot_nt(a, b):
    return lax.dot_general(a, b, (((1,), (1,)), ((), ())), preferred_element_type=F32)


def kernel(tok_hbm, wp_hbm, wc_ref, r_hbm, adv_ref, len_ref, out_ref,
           rb, tb, wpb, wg, wc, dw, gs, gb, ps, sb,
           loc, r_send, r_recv, wz_send, wz_recv, wx_send, wx_recv, ws_send, ws_recv,
           t_send, t_recv, g_send, g_recv, p_send, p_recv):
    tp, dp = lax.axis_index("tp"), lax.axis_index("dp")
    zl, y = lax.div(tp, NY), lax.rem(tp, NY)
    zh, x, core = lax.div(dp, 8), lax.rem(lax.div(dp, 2), NX), lax.rem(dp, 2)
    z = zh * 2 + zl

    def at(y_=None, x_=None, z_=None, core_=None):
        y_, x_ = y if y_ is None else y_, x if x_ is None else x_
        z_, core_ = z if z_ is None else z_, core if core_ is None else core_
        return {"tp": lax.rem(z_, 2) * NY + y_, "dp": lax.div(z_, 2) * 8 + x_ * 2 + core_}

    def ys(k):
        return lax.rem(y + (k + NY), NY)

    def xs(k):
        return lax.rem(x + (k + NX), NX)

    def zs(k):
        return lax.rem(z + (k + NZ), NZ)

    zpart = zh * 2 + (1 - zl)
    sibling = at(core_=1 - core)
    right, left = at(y_=ys(1)), at(y_=ys(-1))

    def remote(src, dst, send, recv, dev):
        return pltpu.make_async_remote_copy(src_ref=src, dst_ref=dst, send_sem=send, recv_sem=recv,
                                            device_id=dev, device_id_type=pl.DeviceIdType.MESH)

    barrier = pltpu.get_barrier_semaphore()
    peers = [at(y_=ys(k)) for k in range(1, NY)] + [at(z_=zs(k)) for k in range(1, NZ)]
    peers += [at(x_=xs(1)), at(x_=xs(-1)), sibling]
    for peer in peers:
        pl.semaphore_signal(barrier, inc=1, device_id=peer, device_id_type=pl.DeviceIdType.MESH)

    half = pl.ds(pl.multiple_of(zl * SEG, SEG), SEG)
    other = pl.ds(pl.multiple_of((1 - zl) * SEG, SEG), SEG)
    own_r = pltpu.make_async_copy(r_hbm, rb.at[OWN], loc.at[0])
    own_wp = pltpu.make_async_copy(wp_hbm, wpb.at[zl], loc.at[1])
    own_t = pltpu.make_async_copy(tok_hbm.at[:, half], tb.at[zl], loc.at[2])
    own_r.start()
    own_wp.start()
    own_t.start()
    mine = wg.at[zl, zh, x, core]
    mine[...] = jnp.zeros((PAD, COLS), BF16)
    mine[pl.ds(0, ROWS), :] = wc_ref[...]
    pl.semaphore_wait(barrier, len(peers))

    wz = {}
    for k in (1, 7, 2, 6, 3, 5, 4):
        wz[k] = remote(mine, mine, wz_send.at[k], wz_recv.at[k], at(z_=zs(k)))
        wz[k].start()

    def chunk(slot, h):
        return rb.at[slot, pl.ds(h * (TOK // 2), TOK // 2)]

    def slot_of(side, d):
        return OWN if d == 0 else FAR if d == 4 else 2 * (d - 1) + side

    def ring(side, d, h):
        i = 2 * d + h if d < 3 else 6
        return remote(chunk(slot_of(side, d), h), chunk(slot_of(side, d + 1), h),
                      r_send.at[side, i], r_recv.at[side, i], left if side else right)

    own_r.wait()
    rings = []
    for h in range(2):
        for side in range(2):
            c = ring(side, 0, h)
            c.start()
            rings.append(c)

    def forward(d, h):
        for side in range(2):
            ring(side, d - 1, h).wait_recv()
            if d < 3 or h == side:
                c = ring(side, d, h)
                c.start()
                rings.append(c)

    zp = at(z_=zpart)
    send_wp = remote(wp_hbm, wpb.at[zl], t_send.at[0], t_recv.at[0], zp)
    send_t = remote(tok_hbm.at[:, other], tb.at[zl], t_send.at[1], t_recv.at[1], zp)
    send_wp.start()
    send_t.start()

    forward(1, 0)
    forward(1, 1)

    def column(k):
        return wg.at[:, :, xs(k), core]

    for k in range(1, NZ):
        wz[k].wait_recv()
    wx, ws = [], []

    def share(k):
        c = remote(column(k), column(k), ws_send.at[k % NX], ws_recv.at[k % NX], sibling)
        c.start()
        ws.append(c)

    for i, k in enumerate((1, -1)):
        c = remote(column(0), column(0), wx_send.at[i], wx_recv.at[i], at(x_=xs(k)))
        c.start()
        wx.append(c)
    share(0)

    forward(2, 0)
    forward(2, 1)

    for i, k in enumerate((1, -1)):
        wx[i].wait_recv()
        part = wg.at[i, :, xs(-k), core]
        c = remote(part, part, wx_send.at[2 + i], wx_recv.at[2 + i], at(x_=xs(k)))
        c.start()
        wx.append(c)
        share(-k)

    forward(3, 0)
    forward(3, 1)

    wx[2].wait_recv()
    wx[3].wait_recv()
    share(2)
    for c in ws:
        c.wait_recv()

    r_i = lax.broadcasted_iota(jnp.int32, (SLICE, NZH * 8 * PAD), 0)
    q_i = lax.broadcasted_iota(jnp.int32, (SLICE, NZH * 8 * PAD), 1)
    q_r = q_i & (PAD - 1)
    pick = jnp.where((q_r < ROWS) & ((q_i >> 4) * ROWS + q_r == r_i), 1.0, 0.0).astype(BF16)
    for s in range(2):
        rows = wg[s].reshape(NZH * 8 * PAD, COLS)
        wc[pl.ds(s * SLICE, SLICE), :] = jnp.dot(pick, rows, preferred_element_type=F32).astype(BF16)

    gsend = []

    def send_g(slot, k):
        c = remote(gs.at[slot], gb.at[y], g_send.at[k], g_recv.at[k], at(y_=ys(k)))
        c.start()
        gsend.append(c)

    for d in range(1, 4):
        block = rb[2 * (d - 1):2 * d].reshape(2 * TOK, COLS)
        g = dot_nt(block, wc[...]).astype(BF16)
        gs[2 * (d - 1)] = g[:TOK]
        gs[2 * d - 1] = g[TOK:]
        send_g(2 * (d - 1), NY - d)
        send_g(2 * d - 1, d)
    ring(0, 3, 0).wait_recv()
    ring(1, 3, 1).wait_recv()
    g = dot_nt(rb[6:8].reshape(2 * TOK, COLS), wc[...]).astype(BF16)
    gs[FAR] = g[TOK:]
    send_g(FAR, 4)
    gb[y] = g[:TOK]

    own_wp.wait()
    send_wp.wait_recv()
    for s in range(2):
        dw[s] = (wc[pl.ds(s * SLICE, SLICE), :].astype(F32) - wpb[s].astype(F32)).astype(BF16)
    own_t.wait()
    send_t.wait_recv()
    shard_of = [-1, 1, -2, 2, -3, 3, 0, 4]
    psend = []
    for pair in range(4):
        block = rb[2 * pair:2 * pair + 2].reshape(2 * TOK, COLS)
        sums = [jnp.zeros((1, TOK), F32)] * 2
        for s in range(2):
            t = dot_nt(dw[s], block)
            for i in range(2):
                cols = pl.ds(pl.multiple_of(ys(shard_of[2 * pair + i]) * TOK, TOK), TOK)
                prod = t[:, i * TOK:(i + 1) * TOK] * tb[s, :, cols].astype(F32)
                sums[i] = sums[i] + jnp.sum(prod, axis=0, keepdims=True)
        for i in range(2):
            slot, k = 2 * pair + i, shard_of[2 * pair + i] % NY
            row = jnp.broadcast_to(sums[i], (8, TOK))
            if k == 0:
                sb[y] = row
            else:
                ps[slot] = row
                c = remote(ps.at[slot], sb.at[y], p_send.at[k], p_recv.at[k], at(y_=ys(k)))
                c.start()
                psend.append(c)

    pos = tp * TOK + lax.broadcasted_iota(jnp.int32, (8, TOK), 1)
    start = jnp.int32(0)
    shares = jnp.zeros((8, TOK), F32)
    for k in range(8):
        n = len_ref[0, k]
        inside = (pos >= start) & (pos < start + n)
        frac = 1.0 / (8.0 * jnp.broadcast_to(n, (8, TOK)).astype(F32))
        shares = shares + jnp.where(inside, frac, 0.0)
        start = start + n
    base = -LOSS_MULTIPLIER * 2048.0 * shares

    for c in psend:
        c.wait_recv()
    diff = jnp.sum(sb[...], axis=0)
    coef = base * jnp.minimum(jnp.exp(diff), 1.0 + EPS_HIGH) * adv_ref[...]
    coef = jnp.broadcast_to(coef[:1], (TOK, TOK))
    eye = (lax.broadcasted_iota(jnp.int32, (TOK, TOK), 0) == lax.broadcasted_iota(jnp.int32, (TOK, TOK), 1))
    scale = jnp.sum(jnp.where(eye, coef, 0.0), axis=1, keepdims=True)

    for c in gsend:
        c.wait_recv()
    for i in range(NY):
        g = gb[i].astype(F32) * scale
        for s in range(2):
            out_ref[:, (s * NY + i) * SLICE:(s * NY + i + 1) * SLICE] = g[:, s * SLICE:(s + 1) * SLICE].astype(BF16)

    for c in rings + list(wz.values()) + wx + ws + gsend + psend + [send_wp, send_t]:
        c.wait_send()


def local(tokens, proximal_weight, current_weight, readout, advantage, lengths):
    vmem, anywhere = pl.BlockSpec(memory_space=pltpu.VMEM), pl.BlockSpec(memory_space=pl.ANY)
    dma = pltpu.SemaphoreType.DMA
    out = pl.pallas_call(
        kernel,
        out_shape=jax.ShapeDtypeStruct((TOK, OUT), BF16),
        in_specs=[anywhere, anywhere, vmem, anywhere, vmem, pl.BlockSpec(memory_space=pltpu.SMEM)],
        out_specs=vmem,
        scratch_shapes=[
            pltpu.VMEM((8, TOK, COLS), BF16),
            pltpu.VMEM((2, SLICE, SEG), BF16),
            pltpu.VMEM((2, SLICE, COLS), BF16),
            pltpu.VMEM((2, NZH, NX, 2, PAD, COLS), BF16),
            pltpu.VMEM((2 * SLICE, COLS), BF16),
            pltpu.VMEM((2, SLICE, COLS), BF16),
            pltpu.VMEM((8, TOK, 2 * SLICE), BF16),
            pltpu.VMEM((8, TOK, 2 * SLICE), BF16),
            pltpu.VMEM((8, 8, TOK), F32),
            pltpu.VMEM((8, 8, TOK), F32),
            dma((3,)), dma((2, 7)), dma((2, 7)), dma((8,)), dma((8,)), dma((4,)), dma((4,)), dma((4,)), dma((4,)),
            dma((2,)), dma((2,)), dma((8,)), dma((8,)), dma((8,)), dma((8,)),
        ],
        compiler_params=pltpu.CompilerParams(
            collective_id=0, has_side_effects=True, vmem_limit_bytes=48 * 1024 * 1024),
        cost_estimate=pl.CostEstimate(flops=4 * 10**9, bytes_accessed=4 * 10**6, transcendentals=1024),
    )(jnp.swapaxes(tokens[0], 0, 1), proximal_weight, current_weight, readout[0], advantage, lengths)
    return out[None]


def solution(mesh):
    in_specs = (
        P("dp", None, "tp"),
        P("tp", None),
        P(("tp", "dp"), None),
        P("dp", "tp", None),
        P("dp", "tp"),
        P("dp", None),
    )
    return jax.shard_map(local, mesh=mesh, in_specs=in_specs, out_specs=P("dp", "tp", None), check_vma=False)
```

time: 276 us -> 78.8 us (0.29)
  waiting for transfers between devices: 92.7 us -> 0 us
  blocking collectives: 85.6 us -> 0 us
  Pallas kernels: 0 us -> 72 us
  other arithmetic: 34.7 us -> 0 us
  local copies, waits for them, and re-layouts: 25.2 us -> 6.48 us
  matrix products: 15.5 us -> 0 us
  between operations: 14.2 us -> 0.02 us
  starting transfers between devices: 7.39 us -> 0 us
    pallas_call x0 -> x1, Pallas kernels: none -> 72 us  [local(): pl.pallas_call(kernel, out_shape=jax.ShapeDtypeStruct((TOK, OUT), BF16),...]
    all_gather x1 -> x0, blocking collectives: 55.9 us -> none  [local(): feature_rows = lax.all_gather(current_weight, 'dp', axis=0, tiled=True)]
    all_gather x2 -> x0, waiting for transfers between devices: 52.3 us -> none  [the longest x1 52.3 us: local(): lax.all_gather(feature_rows, 'tp', axis=0, tiled=True)]
    all_to_all x1 -> x0, waiting for transfers between devices: 40.3 us -> none  [local(): lax.all_to_all(tokens, 'tp', split_axis=1, concat_axis=2, tiled=True)[0]]
    unnamed x1 -> x0, other arithmetic: 34.4 us -> none
    unnamed x1 -> x0, blocking collectives: 29.7 us -> none
    unnamed x20 -> x13, local copies, waits for them, and re-layouts: 23.6 us -> 6.48 us
    dot_general x3 -> x0, matrix products: 15.5 us -> none  [the longest x1 5.75 us: local(): jnp.dot(own_tokens, lax.all_gather(feature_rows, 'tp', axis=0, tiled=True...]
  transfers between devices with their start and end apart: 3 -> 0, of which waited for: 2 -> 0; matrix products, arithmetic and copies ran while one was open for 22% -> 0% of each run, Pallas kernels for 0% -> 0%
where the time goes in v1:
time: 78.8 us; the launch traced here: 78.5 us
  Pallas kernels  72 us (91%)
  local copies, waits for them, and re-layouts  6.48 us (8%)
    pallas_call x1, Pallas kernels, local(): pl.pallas_call(kernel, out_shape=jax.ShapeDtypeStruct((TOK, OUT), BF16),...  72 us
    unnamed x13, local copies, waits for them, and re-layouts  6.48 us

profile of v1, /device:TPU:1, one launch (start us, length us, event | category | flops | bytes accessed | tf_op | source)
XLA Modules:
  0.0 78.5 jit_solution(4742077455439639801)
XLA Ops:
  0.0 0.0 copy-start
  0.0 1.3 %copy-done = bf16[1,2048,320]{1,2,0:T(8,128)(2,1)S(1)} copy-done((bf16[1,2048,320]{1,2,0:T(8,128)(2,1)S(1)}, bf16[1,2048,320]{1,2,0:T(8,128)(2,1)}, u32[]{:S(2)}) %copy-start) | copy-done | bytes 1310744
  1.3 0.0 copy-start.1
  1.3 1.1 %copy-done.1 = bf16[320,1024]{1,0:T(8,128)(2,1)S(1)} copy-done((bf16[320,1024]{1,0:T(8,128)(2,1)S(1)}, bf16[320,1024]{1,0:T(8,128)(2,1)}, u32[]{:S(2)}) %copy-start.1) | copy-done | bytes 655384
  2.4 0.0 copy-start.2
  2.4 0.9 %copy-done.2 = bf16[1,128,1024]{2,1,0:T(8,128)(2,1)S(1)} copy-done((bf16[1,128,1024]{2,1,0:T(8,128)(2,1)S(1)}, bf16[1,128,1024]{2,1,0:T(8,128)(2,1)}, u32[]{:S(2)}) %copy-start.2) | copy-done | bytes 262168
  3.4 0.0 copy-start.3
  3.4 0.8 copy-done.3
  4.1 0.0 copy-start.4
  4.1 0.7 copy-done.4
  4.8 0.0 copy-start.5
  4.8 0.7 copy-done.5
  5.4 72.0 %shard_map.64 = bf16[128,5120]{1,0:T(8,128)(2,1)S(1)} custom-call(bf16[320,2048]{1,0:T(8,128)(2,1)S(1)} %bitcast.6, bf16[320,1024]{1,0:T(8,128)(2,1)S(1)} %copy-done.1, bf16[10,1024]{1,0:T(8,128)(2,1)S(1)} %copy-done.3, bf16[128,1024]{1,0:T(8,128)(2,1)S(1)} %bitcast.7, f32[1,128]{1,0:T(1,128)S(1)} %copy-done.4, s32[1,8]{1,0:T(1,128)S(1)} %copy-done.5), custom_call_target="tpu_custom_call" | custom-call | flops 4000000000 | bytes 4000000 | tf_op jit(solution)/shard_map/pallas_call | solution.py:241
  77.4 1.1 %copy.8 = bf16[1,128,5120]{2,1,0:T(8,128)(2,1)} copy(bf16[1,128,5120]{2,1,0:T(8,128)(2,1)S(1)} %bitcast.5) | data formatting | bytes 2621440
Async XLA Ops:
  0.0 1.3 %copy-start = (bf16[1,2048,320]{1,2,0:T(8,128)(2,1)S(1)}, bf16[1,2048,320]{1,2,0:T(8,128)(2,1)}, u32[]{:S(2)}) copy-start(bf16[1,2048,320]{1,2,0:T(8,128)(2,1)} %param.6) | copy-start | bytes 3932164
  1.3 1.1 %copy-start.1 = (bf16[320,1024]{1,0:T(8,128)(2,1)S(1)}, bf16[320,1024]{1,0:T(8,128)(2,1)}, u32[]{:S(2)}) copy-start(bf16[320,1024]{1,0:T(8,128)(2,1)} %wp_hbm.1) | copy-start | bytes 1966084
  2.4 0.9 %copy-start.2 = (bf16[1,128,1024]{2,1,0:T(8,128)(2,1)S(1)}, bf16[1,128,1024]{2,1,0:T(8,128)(2,1)}, u32[]{:S(2)}) copy-start(bf16[1,128,1024]{2,1,0:T(8,128)(2,1)} %param.9) | copy-start | bytes 786436
  3.4 0.8 copy-start.3
  4.1 0.7 copy-start.4
  4.8 0.7 copy-start.5

commit v2 on v1

v2 whole, which is shorter than its diff:
```python
import jax
import jax.numpy as jnp
from jax import lax
from jax.experimental import pallas as pl
from jax.experimental.pallas import tpu as pltpu
from jax.sharding import PartitionSpec as P

EPS_HIGH = 0.28
LOSS_MULTIPLIER = 64.0
BF16, F32 = jnp.bfloat16, jnp.float32

NX, NY, NZ, NZH = 4, 8, 8, 4
OWN, FAR = 6, 7
TOK, SEG, COLS, SLICE, OUT = 128, 1024, 1024, 320, 5120
ROWS, PAD = 10, 16
COL = NZ * ROWS
AWAY = (3, 4, 5)
FROWS = 32
FALL = NZH * NX * 2 * FROWS
VMEM_LIMIT = 60 * 1024 * 1024


def dot_nt(a, b):
    return lax.dot_general(a, b, (((1,), (1,)), ((), ())), preferred_element_type=F32)


def tenth(v):
    return (v * 6554) >> 16


def iota2(rows, cols):
    return lax.broadcasted_iota(jnp.int32, (rows, cols), 0), lax.broadcasted_iota(jnp.int32, (rows, cols), 1)


def one_where(mask):
    return jnp.where(mask, 1.0, 0.0).astype(BF16)


def kernel(tok_hbm, wp_hbm, wc_hbm, r_hbm, adv_hbm, len_hbm, out_ref,
           rb, tb, wpb, wz_b, wcol, wc, dw, jump, wfar, pick_far, gs, gb, ps, sb, wc_own, adv, lens,
           loc, r_send, r_recv, wz_send, wz_recv, wx_send, wx_recv, ws_send, ws_recv,
           t_send, t_recv, g_send, g_recv, p_send, p_recv,
           j_send, j_recv, fz_send, fz_recv, fx_send, fx_recv, fs_send, fs_recv):
    tp, dp = lax.axis_index("tp"), lax.axis_index("dp")
    zl, y = lax.div(tp, NY), lax.rem(tp, NY)
    zh, x, core = lax.div(dp, 8), lax.rem(lax.div(dp, 2), NX), lax.rem(dp, 2)
    z = zh * 2 + zl

    def at(y_=None, x_=None, z_=None, core_=None):
        y_, x_ = y if y_ is None else y_, x if x_ is None else x_
        z_, core_ = z if z_ is None else z_, core if core_ is None else core_
        return {"tp": lax.rem(z_, 2) * NY + y_, "dp": lax.div(z_, 2) * 8 + x_ * 2 + core_}

    def ys(k):
        return lax.rem(y + (k + NY), NY)

    def xs(k):
        return lax.rem(x + (k + NX), NX)

    def zs(k):
        return lax.rem(z + (k + NZ), NZ)

    sibling = at(core_=1 - core)
    right, left = at(y_=ys(1)), at(y_=ys(-1))
    up, down = at(z_=zs(1)), at(z_=zs(-1))
    started = []

    def remote(src, dst, send, recv, dev):
        return pltpu.make_async_remote_copy(src_ref=src, dst_ref=dst, send_sem=send, recv_sem=recv,
                                            device_id=dev, device_id_type=pl.DeviceIdType.MESH)

    def go(copy):
        copy.start()
        started.append(copy)
        return copy

    barrier = pltpu.get_barrier_semaphore()
    peers = [at(y_=ys(k)) for k in range(1, NY)] + [at(z_=zs(k)) for k in range(1, NZ)]
    peers += [at(x_=xs(1)), at(x_=xs(-1)), sibling]
    for peer in peers:
        pl.semaphore_signal(barrier, inc=1, device_id=peer, device_id_type=pl.DeviceIdType.MESH)

    half = pl.ds(pl.multiple_of(zl * SEG, SEG), SEG)
    other = pl.ds(pl.multiple_of((1 - zl) * SEG, SEG), SEG)
    loads = [pltpu.make_async_copy(src, dst, loc.at[i]) for i, (src, dst) in enumerate((
        (wc_hbm, wc_own), (r_hbm, rb.at[OWN]), (wp_hbm, wpb.at[zl]), (tok_hbm.at[:, half], tb.at[zl]),
        (adv_hbm, adv), (len_hbm, lens)))]
    for load in loads:
        load.start()
    mine = wz_b.at[z]
    mine[...] = jnp.zeros((PAD, COLS), BF16)
    loads[0].wait()
    mine[pl.ds(0, ROWS), :] = wc_own[...]
    loads[1].wait()
    pl.semaphore_wait(barrier, len(peers))

    wz = {}
    for k in (1, 7, 2, 6, 3, 5, 4):
        wz[k] = go(remote(mine, mine, wz_send.at[k], wz_recv.at[k], at(z_=zs(k))))
    jumps = [go(remote(mine, jump.at[i], j_send.at[i], j_recv.at[i], at(y_=ys(-k)))) for i, k in enumerate(AWAY)]

    def chunk(slot, h):
        return rb.at[slot, pl.ds(h * (TOK // 2), TOK // 2)]

    def slot_of(side, d):
        return OWN if d == 0 else FAR if d == 4 else 2 * (d - 1) + side

    def ring(side, d, h):
        i = 2 * d + h if d < 3 else 6
        return remote(chunk(slot_of(side, d), h), chunk(slot_of(side, d + 1), h),
                      r_send.at[side, i], r_recv.at[side, i], left if side else right)

    for h in range(2):
        for side in range(2):
            go(ring(side, 0, h))

    def forward(d):
        for h in range(2):
            for side in range(2):
                ring(side, d - 1, h).wait_recv()
                if d < 3 or h == side:
                    go(ring(side, d, h))

    def far_block(zz, part=None):
        ref = wfar.at[lax.rem(zz, 2), lax.div(zz, 2), x, core]
        return ref if part is None else ref.at[pl.ds(part * PAD, PAD)]

    def far_ring(side, d):
        block = far_block(zs(d if side else -d), side if d == 3 else None)
        return remote(block, block, fz_send.at[side, d], fz_recv.at[side, d], down if side else up)

    def far_came(side, d):
        block = far_block(zs((d + 1) if side else -(d + 1)), side if d == 3 else None)
        remote(block, block, fz_send.at[side, d], fz_recv.at[side, d], down if side else up).wait_recv()

    t_i, q_i = iota2(FROWS, 3 * PAD)
    pack = one_where((t_i < 3 * ROWS) & (tenth(t_i) * PAD + t_i - tenth(t_i) * ROWS == q_i))
    for c in jumps:
        c.wait_recv()
    wfar[zl, zh, x, core] = jnp.dot(
        pack, jump[...].reshape(3 * PAD, COLS), preferred_element_type=F32).astype(BF16)
    for side in range(2):
        go(far_ring(side, 0))

    zp = at(z_=zh * 2 + (1 - zl))
    wp_part = pl.ds(pl.multiple_of(core * (SLICE // 2), SLICE // 2), SLICE // 2)
    send_wp = go(remote(wp_hbm.at[wp_part], wpb.at[zl, wp_part], t_send.at[0], t_recv.at[0], zp))
    send_t = go(remote(tok_hbm.at[:, other], tb.at[zl], t_send.at[1], t_recv.at[1], zp))

    forward(1)
    for side in range(2):
        far_came(side, 0)
        go(far_ring(side, 1))

    t_i, q_i = iota2(COL, NZ * PAD)
    t_b = tenth(t_i)
    pick_col = one_where((2 * (t_b & (NZH - 1)) + (t_b >> 2)) * PAD + t_i - t_b * ROWS == q_i)
    for k in range(1, NZ):
        wz[k].wait_recv()
    wcol[x, core] = jnp.dot(
        pick_col, wz_b[...].reshape(NZ * PAD, COLS), preferred_element_type=F32).astype(BF16)

    def spread(buf, sends, recvs, sib_sends, sib_recvs, parts):
        def share(k):
            block = buf(xs(k), None)
            return go(remote(block, block, sib_sends.at[k % NX], sib_recvs.at[k % NX], sibling))

        own = [go(remote(buf(x, None), buf(x, None), sends.at[i], recvs.at[i], at(x_=xs(k))))
               for i, k in enumerate((1, -1))]
        shares = [share(0)]

        def second():
            for i, k in enumerate((1, -1)):
                own[i].wait_recv()
                block = buf(xs(-k), parts[i])
                own.append(go(remote(block, block, sends.at[2 + i], recvs.at[2 + i], at(x_=xs(k)))))
                shares.append(share(-k))

        def third():
            own[2].wait_recv()
            own[3].wait_recv()
            shares.append(share(2))

        def last():
            for c in shares:
                c.wait_recv()

        return second, third, last

    def near_buf(xx, part):
        ref = wcol.at[xx, core]
        return ref if part is None else ref.at[pl.ds(*part)]

    near = spread(near_buf, wx_send, wx_recv, ws_send, ws_recv, ((0, 48), (48, 32)))

    forward(2)
    for side in range(2):
        far_came(side, 1)
        go(far_ring(side, 2))
    near[0]()
    forward(3)
    for side in range(2):
        far_came(side, 2)
        go(far_ring(side, 3))
    near[1]()

    r_i, q_i = iota2(2 * SLICE, NX * 2 * COL)
    r_s = jnp.where(r_i >= SLICE, 1, 0)
    r_f = r_i - r_s * SLICE
    r_b = tenth(r_f)
    pick = one_where((r_b & 7) * COL + (r_s * NZH + (r_b >> 3)) * ROWS + r_f - r_b * ROWS == q_i)
    near[2]()
    wc[...] = jnp.dot(pick, wcol[...].reshape(NX * 2 * COL, COLS), preferred_element_type=F32).astype(BF16)

    gsend = []

    def send_g(slot, k):
        gsend.append(go(remote(gs.at[slot], gb.at[y], g_send.at[k], g_recv.at[k], at(y_=ys(k)))))

    for d in range(1, 3):
        block = rb[2 * (d - 1):2 * d].reshape(2 * TOK, COLS)
        g = dot_nt(block, wc[...]).astype(BF16)
        gs[2 * (d - 1)] = g[:TOK]
        gs[2 * d - 1] = g[TOK:]
        send_g(2 * (d - 1), NY - d)
        send_g(2 * d - 1, d)

    for side in range(2):
        far_came(side, 3)

    def far_buf(xx, part):
        return wfar.at[:, :, xx, core] if part is None else wfar.at[part, :, xx, core]

    far = spread(far_buf, fx_send, fx_recv, fs_send, fs_recv, (0, 1))

    ring(0, 3, 0).wait_recv()
    ring(1, 3, 1).wait_recv()
    loads[2].wait()
    send_wp.wait_recv()
    share_wp = go(remote(wpb.at[1 - zl, wp_part], wpb.at[1 - zl, wp_part], t_send.at[2], t_recv.at[2], sibling))
    gb[y] = dot_nt(rb[OWN], wc[...]).astype(BF16)

    q_i, f_i = iota2(FALL, SLICE)
    q_r = q_i & (FROWS - 1)
    for i in range(3):
        q_f = q_r - i * ROWS
        pick_far[i] = one_where((q_f >= 0) & (q_f < ROWS) & ((q_i >> 5) * ROWS + q_f == f_i))

    share_wp.wait_recv()
    for s in range(2):
        dw[s] = (wc[pl.ds(s * SLICE, SLICE), :].astype(F32) - wpb[s].astype(F32)).astype(BF16)
    loads[3].wait()
    send_t.wait_recv()
    far[0]()
    shard_of = [-1, 1, -2, 2, -3, 3, 0, 4]
    psend = []
    for pair in range(4):
        block = rb[2 * pair:2 * pair + 2].reshape(2 * TOK, COLS)
        sums = [jnp.zeros((1, TOK), F32)] * 2
        for s in range(2):
            t = dot_nt(dw[s], block)
            for i in range(2):
                cols = pl.ds(pl.multiple_of(ys(shard_of[2 * pair + i]) * TOK, TOK), TOK)
                prod = t[:, i * TOK:(i + 1) * TOK] * tb[s, :, cols].astype(F32)
                sums[i] = sums[i] + jnp.sum(prod, axis=0, keepdims=True)
        for i in range(2):
            slot, k = 2 * pair + i, shard_of[2 * pair + i] % NY
            row = jnp.broadcast_to(sums[i], (8, TOK))
            if k == 0:
                sb[y] = row
            else:
                ps[slot] = row
                psend.append(go(remote(ps.at[slot], sb.at[y], p_send.at[k], p_recv.at[k], at(y_=ys(k)))))

    loads[4].wait()
    loads[5].wait()
    pos = tp * TOK + lax.broadcasted_iota(jnp.int32, (8, TOK), 1)
    start = jnp.int32(0)
    shares = jnp.zeros((8, TOK), F32)
    for k in range(8):
        n = lens[0, k]
        inside = (pos >= start) & (pos < start + n)
        frac = 1.0 / (8.0 * jnp.broadcast_to(n, (8, TOK)).astype(F32))
        shares = shares + jnp.where(inside, frac, 0.0)
        start = start + n
    base = -LOSS_MULTIPLIER * 2048.0 * shares

    for c in psend:
        c.wait_recv()
    diff = jnp.sum(sb[...], axis=0)
    coef = base * jnp.minimum(jnp.exp(diff), 1.0 + EPS_HIGH) * adv[...]
    coef = jnp.broadcast_to(coef[:1], (TOK, TOK))
    t_i, q_i = iota2(TOK, TOK)
    scale = jnp.sum(jnp.where(t_i == q_i, coef, 0.0), axis=1, keepdims=True)

    far[1]()
    far[2]()
    for s in range(2):
        g = dot_nt(rb[OWN], wfar[s].reshape(FALL, COLS)).astype(BF16)
        for i, k in enumerate(AWAY):
            part = jnp.dot(g, pick_far[i], preferred_element_type=F32)
            gb[ys(k), :, s * SLICE:(s + 1) * SLICE] = part.astype(BF16)

    for c in gsend:
        c.wait_recv()
    for i in range(NY):
        g = gb[i].astype(F32) * scale
        for s in range(2):
            out_ref[:, (s * NY + i) * SLICE:(s * NY + i + 1) * SLICE] = g[:, s * SLICE:(s + 1) * SLICE].astype(BF16)

    for c in started:
        c.wait_send()


def local(tokens, proximal_weight, current_weight, readout, advantage, lengths):
    anywhere = pl.BlockSpec(memory_space=pl.ANY)
    dma, vmem = pltpu.SemaphoreType.DMA, pltpu.VMEM
    out = pl.pallas_call(
        kernel,
        out_shape=jax.ShapeDtypeStruct((TOK, OUT), BF16),
        in_specs=[anywhere] * 6,
        out_specs=pl.BlockSpec(memory_space=vmem),
        scratch_shapes=[
            vmem((8, TOK, COLS), BF16),
            vmem((2, SLICE, SEG), BF16),
            vmem((2, SLICE, COLS), BF16),
            vmem((NZ, PAD, COLS), BF16),
            vmem((NX, 2, COL, COLS), BF16),
            vmem((2 * SLICE, COLS), BF16),
            vmem((2, SLICE, COLS), BF16),
            vmem((3, PAD, COLS), BF16),
            vmem((2, NZH, NX, 2, FROWS, COLS), BF16),
            vmem((3, FALL, SLICE), BF16),
            vmem((4, TOK, 2 * SLICE), BF16),
            vmem((8, TOK, 2 * SLICE), BF16),
            vmem((8, 8, TOK), F32),
            vmem((8, 8, TOK), F32),
            vmem((ROWS, COLS), BF16),
            vmem((1, TOK), F32),
            pltpu.SMEM((1, 8), jnp.int32),
            dma((6,)), dma((2, 7)), dma((2, 7)), dma((8,)), dma((8,)), dma((4,)), dma((4,)), dma((4,)), dma((4,)),
            dma((3,)), dma((3,)), dma((8,)), dma((8,)), dma((8,)), dma((8,)),
            dma((3,)), dma((3,)), dma((2, 4)), dma((2, 4)), dma((4,)), dma((4,)), dma((4,)), dma((4,)),
        ],
        compiler_params=pltpu.CompilerParams(
            collective_id=0, has_side_effects=True, vmem_limit_bytes=VMEM_LIMIT),
        cost_estimate=pl.CostEstimate(flops=5 * 10**9, bytes_accessed=4 * 10**6, transcendentals=1024),
    )(jnp.swapaxes(tokens[0], 0, 1), proximal_weight, current_weight, readout[0], advantage, lengths)
    return out[None]


def solution(mesh):
    in_specs = (
        P("dp", None, "tp"),
        P("tp", None),
        P(("tp", "dp"), None),
        P("dp", "tp", None),
        P("dp", "tp"),
        P("dp", None),
    )
    return jax.shard_map(local, mesh=mesh, in_specs=in_specs, out_specs=P("dp", "tp", None), check_vma=False)
```

time: 78.8 us -> 85.2 us (1.081)
  Pallas kernels: 72 us -> 82.6 us
  local copies, waits for them, and re-layouts: 6.48 us -> 2.46 us
    pallas_call x1, Pallas kernels: 72 us -> 82.6 us  [local(): pl.pallas_call(kernel, out_shape=jax.ShapeDtypeStruct((TOK, OUT), BF16),...]
    unnamed x13 -> x1, local copies, waits for them, and re-layouts: 6.48 us -> 2.46 us
where the time goes in v2:
time: 85.2 us; the launch traced here: 85.1 us
  Pallas kernels  82.6 us (97%)
  local copies, waits for them, and re-layouts  2.46 us (3%)
    pallas_call x1, Pallas kernels, local(): pl.pallas_call(kernel, out_shape=jax.ShapeDtypeStruct((TOK, OUT), BF16),...  82.6 us
    unnamed x1, local copies, waits for them, and re-layouts  2.46 us

profile of v2, /device:TPU:1, one launch (start us, length us, event | category | flops | bytes accessed | tf_op | source)
XLA Modules:
  0.0 85.1 jit_solution(7398683364368195244)
XLA Ops:
  0.0 82.6 %shard_map.64 = bf16[128,5120]{1,0:T(8,128)(2,1)} custom-call(bf16[320,2048]{1,0:T(8,128)(2,1)} %bitcast.6, bf16[320,1024]{1,0:T(8,128)(2,1)} %wp_hbm.1, bf16[10,1024]{1,0:T(8,128)(2,1)} %wc_hbm.1, bf16[128,1024]{1,0:T(8,128)(2,1)} %bitcast.7, f32[1,128]{1,0:T(1,128)} %adv_hbm.1, s32[1,8]{1,0:T(1,128)} %len_hbm.1), custom_call_target="tpu_custom_call" | custom-call | flops 5000000000 | bytes 4000000 | tf_op jit(solution)/shard_map/pallas_call | solution.py:318
  82.6 2.5 %copy.8 = bf16[1,128,5120]{2,1,0:T(8,128)(2,1)} copy(bf16[1,128,5120]{2,1,0:T(8,128)(2,1)} %bitcast.5) | data formatting | bytes 2621440

commit v3 on v2

v3 whole, which is shorter than its diff:
```python
import jax
import jax.numpy as jnp
from jax import lax
from jax.experimental import pallas as pl
from jax.experimental.pallas import tpu as pltpu
from jax.sharding import PartitionSpec as P

EPS_HIGH = 0.28
LOSS_MULTIPLIER = 64.0
BF16, F32 = jnp.bfloat16, jnp.float32

NX, NY, NZ, NZH = 4, 8, 8, 4
OWN, FAR = 6, 7
TOK, SEG, COLS, SLICE, OUT = 128, 1024, 1024, 320, 5120
ROWS, PAD = 10, 16
COL = NZ * ROWS
VMEM_LIMIT = 60 * 1024 * 1024


def dot_nt(a, b):
    return lax.dot_general(a, b, (((1,), (1,)), ((), ())), preferred_element_type=F32)


def tenth(v):
    return (v * 6554) >> 16


def rows_of(n):
    return lax.broadcasted_iota(jnp.int32, (n, 1), 0)


def ones_at(column, cols):
    shape = (column.shape[0], cols)
    at = jnp.broadcast_to(column, shape) == lax.broadcasted_iota(jnp.int32, shape, 1)
    return jnp.where(at, 1.0, 0.0).astype(BF16)


def kernel(tok_hbm, wp_hbm, wc_hbm, r_hbm, adv_hbm, len_hbm, out_ref,
           rb, tb, wpb, wz_b, wcol, wc, dw, pick, gs, gb, ps, sb, wc_own, adv, lens,
           loc, r_send, r_recv, wz_send, wz_recv, wx_send, wx_recv, ws_send, ws_recv,
           t_send, t_recv, g_send, g_recv, p_send, p_recv, j_send, j_recv):
    tp, dp = lax.axis_index("tp"), lax.axis_index("dp")
    zl, y = lax.div(tp, NY), lax.rem(tp, NY)
    zh, x, core = lax.div(dp, 8), lax.rem(lax.div(dp, 2), NX), lax.rem(dp, 2)
    z = zh * 2 + zl

    def at(y_=None, x_=None, z_=None, core_=None):
        y_, x_ = y if y_ is None else y_, x if x_ is None else x_
        z_, core_ = z if z_ is None else z_, core if core_ is None else core_
        return {"tp": lax.rem(z_, 2) * NY + y_, "dp": lax.div(z_, 2) * 8 + x_ * 2 + core_}

    def ys(k):
        return lax.rem(y + (k + NY), NY)

    def xs(k):
        return lax.rem(x + (k + NX), NX)

    sibling = at(core_=1 - core)
    right, left = at(y_=ys(1)), at(y_=ys(-1))
    partner = at(z_=zh * 2 + (1 - zl))
    started = []

    def remote(src, dst, send, recv, dev):
        return pltpu.make_async_remote_copy(src_ref=src, dst_ref=dst, send_sem=send, recv_sem=recv,
                                            device_id=dev, device_id_type=pl.DeviceIdType.MESH)

    def go(copy):
        copy.start()
        started.append(copy)
        return copy

    barrier = pltpu.get_barrier_semaphore()
    peers = [at(y_=ys(k)) for k in range(1, NY)] + [at(x_=xs(1)), at(x_=xs(-1)), sibling]

    def greet(peer):
        pl.semaphore_signal(barrier, inc=1, device_id=peer, device_id_type=pl.DeviceIdType.MESH)

    for peer in peers:
        greet(peer)
    for j in range(NZ):
        @pl.when(z < j)
        def _():
            greet(at(z_=j))

    half = pl.ds(pl.multiple_of(zl * SEG, SEG), SEG)
    other = pl.ds(pl.multiple_of((1 - zl) * SEG, SEG), SEG)
    loads = [pltpu.make_async_copy(src, dst, loc.at[i]) for i, (src, dst) in enumerate((
        (wc_hbm, wc_own), (r_hbm, rb.at[OWN]), (wp_hbm, wpb.at[zl]), (tok_hbm.at[:, half], tb.at[zl]),
        (adv_hbm, adv), (len_hbm, lens)))]
    for load in loads:
        load.start()
    mine = wz_b.at[0, z]
    mine[...] = jnp.zeros((PAD, COLS), BF16)
    loads[0].wait()
    mine[pl.ds(0, ROWS), :] = wc_own[...]
    loads[1].wait()
    pl.semaphore_wait(barrier, len(peers) + z)

    def give(w, to):
        block = wz_b.at[w, z]
        return remote(block, block, wz_send.at[w, to], wz_recv.at[w, z], at(z_=to))

    def came(w, b):
        block = wz_b.at[w, b]
        remote(block, block, wz_send.at[w, b], wz_recv.at[w, b], sibling).wait_recv()

    def lower(w):
        for k in range(1, NZ):
            @pl.when(k <= z)
            def _():
                give(w, z - k).start()

    def higher(w, *steps):
        for k in steps:
            @pl.when(z + k < NZ)
            def _():
                if w == 0:
                    came(w, z + k)
                give(w, z + k).start()

    def gathered(w):
        for b in range(NZ):
            @pl.when((b < z) if w == 0 else (b != z))
            def _():
                came(w, b)

    def settle(w):
        for b in range(NZ):
            @pl.when(b != z)
            def _():
                give(w, b).wait_send()

    lower(0)

    def chunk(slot, h):
        return rb.at[slot, pl.ds(h * (TOK // 2), TOK // 2)]

    def slot_of(side, d):
        return OWN if d == 0 else FAR if d == 4 else 2 * (d - 1) + side

    def ring(side, d, h):
        i = 2 * d + h if d < 3 else 6
        return remote(chunk(slot_of(side, d), h), chunk(slot_of(side, d + 1), h),
                      r_send.at[side, i], r_recv.at[side, i], left if side else right)

    go(ring(0, 0, 0))
    go(ring(1, 0, 0))
    jump = go(remote(mine, wz_b.at[1, z], j_send, j_recv, at(y_=ys(4))))
    go(ring(0, 0, 1))
    go(ring(1, 0, 1))

    def forward(d, h):
        for side in range(2):
            ring(side, d - 1, h).wait_recv()
            if d < 3 or h == side:
                go(ring(side, d, h))

    t_i = rows_of(COL)
    t_b = tenth(t_i)
    pick_col = ones_at((2 * (t_b & (NZH - 1)) + (t_b >> 2)) * PAD + t_i - t_b * ROWS, NZ * PAD)
    r_i = rows_of(2 * SLICE)
    r_s = jnp.where(r_i >= SLICE, 1, 0)
    r_f = r_i - r_s * SLICE
    r_b = tenth(r_f)
    pick[...] = ones_at((r_b & 7) * COL + (r_s * NZH + (r_b >> 3)) * ROWS + r_f - r_b * ROWS, NX * 2 * COL)

    higher(0, 1, 2)
    forward(1, 0)
    higher(0, 3, 4)
    forward(1, 1)
    higher(0, 5, 6, 7)
    jump.wait_recv()

    def spread(w):
        def block(k, part=None):
            ref = wcol.at[w, xs(k), core]
            return ref if part is None else ref.at[pl.ds(*part)]

        def over(i, k, src):
            return go(remote(src, src, wx_send.at[w, i], wx_recv.at[w, i], at(x_=xs(k))))

        def share(k):
            shares.append(go(remote(block(k), block(k), ws_send.at[w, k % NX], ws_recv.at[w, k % NX], sibling)))

        own, shares = [], []

        def first():
            gathered(w)
            wcol[w, x, core] = jnp.dot(
                pick_col, wz_b[w].reshape(NZ * PAD, COLS), preferred_element_type=F32).astype(BF16)
            own.extend(over(i, k, block(0)) for i, k in enumerate((1, -1)))
            share(0)

        def second():
            for i, (k, part) in enumerate(((1, (0, 48)), (-1, (48, 32)))):
                own[i].wait_recv()
                own.append(over(2 + i, k, block(-k, part)))
                share(-k)

        def third():
            own[2].wait_recv()
            own[3].wait_recv()
            share(2)

        def last():
            for c in shares:
                c.wait_recv()
            wc[w] = jnp.dot(
                pick[...], wcol[w].reshape(NX * 2 * COL, COLS), preferred_element_type=F32).astype(BF16)

        return first, second, third, last

    near, far = spread(0), spread(1)
    near[0]()
    forward(2, 0)
    lower(1)
    higher(1, *range(1, NZ))
    wp_part = pl.ds(pl.multiple_of(core * (SLICE // 2), SLICE // 2), SLICE // 2)
    send_wp = go(remote(wp_hbm.at[wp_part], wpb.at[zl, wp_part], t_send.at[0], t_recv.at[0], partner))
    send_t = go(remote(tok_hbm.at[:, other], tb.at[zl], t_send.at[1], t_recv.at[1], partner))
    forward(2, 1)
    near[1]()
    forward(3, 0)
    near[2]()
    near[3]()

    gsend = []

    def send_g(slot, k):
        gsend.append(go(remote(gs.at[slot], gb.at[y], g_send.at[k], g_recv.at[k], at(y_=ys(k)))))

    def gradient(d):
        block = rb[2 * (d - 1):2 * d].reshape(2 * TOK, COLS)
        g = dot_nt(block, wc[0]).astype(BF16)
        gs[2 * (d - 1)] = g[:TOK]
        gs[2 * d - 1] = g[TOK:]
        send_g(2 * (d - 1), NY - d)
        send_g(2 * d - 1, d)

    gradient(1)
    forward(3, 1)
    gradient(2)
    gradient(3)
    far[0]()
    loads[2].wait()
    send_wp.wait_recv()
    share_wp = go(remote(wpb.at[1 - zl, wp_part], wpb.at[1 - zl, wp_part], t_send.at[2], t_recv.at[2], sibling))

    share_wp.wait_recv()
    for s in range(2):
        dw[s] = (wc[0, pl.ds(s * SLICE, SLICE), :].astype(F32) - wpb[s].astype(F32)).astype(BF16)
    ring(0, 3, 0).wait_recv()
    ring(1, 3, 1).wait_recv()
    shard_of = [-1, 1, -2, 2, -3, 3, 0, 4]

    def scores(s, pair):
        t = dot_nt(dw[s], rb[2 * pair:2 * pair + 2].reshape(2 * TOK, COLS))
        sums = []
        for i in range(2):
            cols = pl.ds(pl.multiple_of(ys(shard_of[2 * pair + i]) * TOK, TOK), TOK)
            prod = t[:, i * TOK:(i + 1) * TOK] * tb[s, :, cols].astype(F32)
            sums.append(jnp.sum(prod, axis=0, keepdims=True))
        return sums

    loads[3].wait()
    first = [scores(zl, pair) for pair in range(4)]
    gb[y] = dot_nt(rb[OWN], wc[0]).astype(BF16)
    far[1]()
    send_t.wait_recv()
    psend = []
    for pair in range(4):
        second = scores(1 - zl, pair)
        for i in range(2):
            slot, k = 2 * pair + i, shard_of[2 * pair + i] % NY
            row = jnp.broadcast_to(first[pair][i] + second[i], (8, TOK))
            if k == 0:
                sb[y] = row
            else:
                ps[slot] = row
                psend.append(go(remote(ps.at[slot], sb.at[y], p_send.at[k], p_recv.at[k], at(y_=ys(k)))))

    loads[4].wait()
    loads[5].wait()
    pos = tp * TOK + lax.broadcasted_iota(jnp.int32, (8, TOK), 1)
    start = jnp.int32(0)
    shares = jnp.zeros((8, TOK), F32)
    for k in range(8):
        n = lens[0, k]
        inside = (pos >= start) & (pos < start + n)
        frac = 1.0 / (8.0 * jnp.broadcast_to(n, (8, TOK)).astype(F32))
        shares = shares + jnp.where(inside, frac, 0.0)
        start = start + n
    base = -LOSS_MULTIPLIER * 2048.0 * shares

    far[2]()
    far[3]()
    gb[ys(4)] = dot_nt(rb[OWN], wc[1]).astype(BF16)

    for c in psend:
        c.wait_recv()
    diff = jnp.sum(sb[...], axis=0)
    coef = base * jnp.minimum(jnp.exp(diff), 1.0 + EPS_HIGH) * adv[...]
    coef = jnp.broadcast_to(coef[:1], (TOK, TOK))
    eye = ones_at(rows_of(TOK), TOK).astype(F32)
    scale = jnp.sum(jnp.where(eye > 0.0, coef, 0.0), axis=1, keepdims=True)

    for c in gsend:
        c.wait_recv()
    for i in range(NY):
        g = gb[i].astype(F32) * scale
        for s in range(2):
            out_ref[:, (s * NY + i) * SLICE:(s * NY + i + 1) * SLICE] = g[:, s * SLICE:(s + 1) * SLICE].astype(BF16)

    for c in started:
        c.wait_send()
    settle(0)
    settle(1)


def local(tokens, proximal_weight, current_weight, readout, advantage, lengths):
    anywhere = pl.BlockSpec(memory_space=pl.ANY)
    dma, vmem = pltpu.SemaphoreType.DMA, pltpu.VMEM
    out = pl.pallas_call(
        kernel,
        out_shape=jax.ShapeDtypeStruct((TOK, OUT), BF16),
        in_specs=[anywhere] * 6,
        out_specs=pl.BlockSpec(memory_space=vmem),
        scratch_shapes=[
            vmem((8, TOK, COLS), BF16),
            vmem((2, SLICE, SEG), BF16),
            vmem((2, SLICE, COLS), BF16),
            vmem((2, NZ, PAD, COLS), BF16),
            vmem((2, NX, 2, COL, COLS), BF16),
            vmem((2, 2 * SLICE, COLS), BF16),
            vmem((2, SLICE, COLS), BF16),
            vmem((2 * SLICE, NX * 2 * COL), BF16),
            vmem((6, TOK, 2 * SLICE), BF16),
            vmem((8, TOK, 2 * SLICE), BF16),
            vmem((8, 8, TOK), F32),
            vmem((8, 8, TOK), F32),
            vmem((ROWS, COLS), BF16),
            vmem((1, TOK), F32),
            pltpu.SMEM((1, 8), jnp.int32),
            dma((6,)), dma((2, 7)), dma((2, 7)), dma((2, 8)), dma((2, 8)),
            dma((2, 4)), dma((2, 4)), dma((2, 4)), dma((2, 4)),
            dma((3,)), dma((3,)), dma((8,)), dma((8,)), dma((8,)), dma((8,)), dma, dma,
        ],
        compiler_params=pltpu.CompilerParams(
            collective_id=0, has_side_effects=True, vmem_limit_bytes=VMEM_LIMIT),
        cost_estimate=pl.CostEstimate(flops=5 * 10**9, bytes_accessed=4 * 10**6, transcendentals=1024),
    )(jnp.swapaxes(tokens[0], 0, 1), proximal_weight, current_weight, readout[0], advantage, lengths)
    return out[None]


def solution(mesh):
    in_specs = (
        P("dp", None, "tp"),
        P("tp", None),
        P(("tp", "dp"), None),
        P("dp", "tp", None),
        P("dp", "tp"),
        P("dp", None),
    )
    return jax.shard_map(local, mesh=mesh, in_specs=in_specs, out_specs=P("dp", "tp", None), check_vma=False)
```

time: 85.2 us -> 67.4 us (0.79)
  Pallas kernels: 82.6 us -> 64.7 us
    pallas_call x1, Pallas kernels: 82.6 us -> 64.7 us  [local(): pl.pallas_call(kernel, out_shape=jax.ShapeDtypeStruct((TOK, OUT), BF16),...]
where the time goes in v3:
time: 67.4 us; the launch traced here: 67.2 us
  Pallas kernels  64.7 us (96%)
  local copies, waits for them, and re-layouts  2.46 us (4%)
    pallas_call x1, Pallas kernels, local(): pl.pallas_call(kernel, out_shape=jax.ShapeDtypeStruct((TOK, OUT), BF16),...  64.7 us
    unnamed x1, local copies, waits for them, and re-layouts  2.46 us

profile of v3, /device:TPU:1, one launch (start us, length us, event | category | flops | bytes accessed | tf_op | source)
XLA Modules:
  0.0 67.2 jit_solution(4533431763216119984)
XLA Ops:
  0.0 64.7 %shard_map.64 = bf16[128,5120]{1,0:T(8,128)(2,1)} custom-call(bf16[320,2048]{1,0:T(8,128)(2,1)} %bitcast.6, bf16[320,1024]{1,0:T(8,128)(2,1)} %wp_hbm.1, bf16[10,1024]{1,0:T(8,128)(2,1)} %wc_hbm.1, bf16[128,1024]{1,0:T(8,128)(2,1)} %bitcast.7, f32[1,128]{1,0:T(1,128)} %adv_hbm.1, s32[1,8]{1,0:T(1,128)} %len_hbm.1), custom_call_target="tpu_custom_call" | custom-call | flops 5000000000 | bytes 4000000 | tf_op jit(solution)/shard_map/pallas_call | solution.py:323
  64.8 2.5 %copy.8 = bf16[1,128,5120]{2,1,0:T(8,128)(2,1)} copy(bf16[1,128,5120]{2,1,0:T(8,128)(2,1)} %bitcast.5) | data formatting | bytes 2621440

commit v4 on v3

--- a/solution.py
+++ b/solution.py
@@ -36,8 +36,8 @@
 
 
 def kernel(tok_hbm, wp_hbm, wc_hbm, r_hbm, adv_hbm, len_hbm, out_ref,
-           rb, tb, wpb, wz_b, wcol, wc, dw, pick, gs, gb, ps, sb, wc_own, adv, lens,
-           loc, r_send, r_recv, wz_send, wz_recv, wx_send, wx_recv, ws_send, ws_recv,
+           rb, tb, wpb, wg, wz_b, wcol, wc, dw, pick, pick_near, gs, gb, ps, sb, wc_own, adv, lens,
+           loc, r_send, r_recv, wz_send, wz_recv, wx_send, wx_recv, ws_send, ws_recv, nx_send, nx_recv, ny_send, ny_recv, ns_send, ns_recv,
            t_send, t_recv, g_send, g_recv, p_send, p_recv, j_send, j_recv):
     tp, dp = lax.axis_index("tp"), lax.axis_index("dp")
     zl, y = lax.div(tp, NY), lax.rem(tp, NY)
@@ -89,48 +89,103 @@
         (adv_hbm, adv), (len_hbm, lens)))]
     for load in loads:
         load.start()
-    mine = wz_b.at[0, z]
+    mine = wg.at[zl, zh, x, core]
     mine[...] = jnp.zeros((PAD, COLS), BF16)
     loads[0].wait()
     mine[pl.ds(0, ROWS), :] = wc_own[...]
     loads[1].wait()
     pl.semaphore_wait(barrier, len(peers) + z)
 
+    def block(w, b):
+        return wz_b.at[b] if w else wg.at[lax.rem(b, 2), lax.div(b, 2), x, core]
+
     def give(w, to):
-        block = wz_b.at[w, z]
-        return remote(block, block, wz_send.at[w, to], wz_recv.at[w, z], at(z_=to))
+        return remote(block(w, z), block(w, z), wz_send.at[w, to], wz_recv.at[w, z], at(z_=to))
 
     def came(w, b):
-        block = wz_b.at[w, b]
-        remote(block, block, wz_send.at[w, b], wz_recv.at[w, b], sibling).wait_recv()
-
-    def lower(w):
+        remote(block(w, b), block(w, b), wz_send.at[w, b], wz_recv.at[w, b], sibling).wait_recv()
+
+    def near_block(b, k):
+        return wg.at[lax.rem(b, 2), lax.div(b, 2), xs(k), core]
+
+    def near_over(b, i):
+        src = near_block(b, 0)
+        return remote(src, src, nx_send.at[i, b], nx_recv.at[i, b], at(x_=xs(-1 if i else 1)))
+
+    def near_on(b, i):
+        src = near_block(b, 1 if i else -1)
+        return remote(src, src, ny_send.at[b], ny_recv.at[b], at(x_=xs(-1 if i else 1)))
+
+    def over(b):
+        for i in range(2):
+            near_over(b, i).start()
+
+    def lower():
         for k in range(1, NZ):
             @pl.when(k <= z)
             def _():
-                give(w, z - k).start()
-
-    def higher(w, *steps):
+                give(0, z - k).start()
+
+    def higher(*steps):
         for k in steps:
             @pl.when(z + k < NZ)
             def _():
-                if w == 0:
-                    came(w, z + k)
-                give(w, z + k).start()
-
-    def gathered(w):
-        for b in range(NZ):
-            @pl.when((b < z) if w == 0 else (b != z))
-            def _():
-                came(w, b)
-
-    def settle(w):
+                came(0, z + k)
+                give(0, z + k).start()
+                over(z + k)
+
+    def from_lower():
+        for k in range(1, NZ):
+            @pl.when(k <= z)
+            def _():
+                came(0, z - k)
+                over(z - k)
+
+    def onward(b):
+        for i in range(2):
+            src = near_block(b, 1 if i else -1)
+            remote(src, src, nx_send.at[i, b], nx_recv.at[i, b], sibling).wait_recv()
+        for i in range(2):
+            @pl.when(lax.rem(b, 2) == i)
+            def _():
+                near_on(b, i).start()
+
+    def onward_lower():
+        for k in range(NZ):
+            @pl.when(k <= z)
+            def _():
+                onward(z - k)
+
+    def onward_higher():
+        for k in range(1, NZ):
+            @pl.when(z + k < NZ)
+            def _():
+                onward(z + k)
+
+    def near_column(k):
+        return wg.at[:, :, xs(k), core]
+
+    def near_share(k):
+        c = remote(near_column(k), near_column(k), ns_send.at[k % NX], ns_recv.at[k % NX], sibling)
+        return go(c)
+
+    def gathered():
         for b in range(NZ):
             @pl.when(b != z)
             def _():
-                give(w, b).wait_send()
-
-    lower(0)
+                came(1, b)
+
+    def settle():
+        for b in range(NZ):
+            @pl.when(b != z)
+            def _():
+                give(0, b).wait_send()
+            for i in range(2):
+                near_over(b, i).wait_send()
+            near_on(b, b % 2).wait_send()
+
+    lower()
+    over(z)
 
     def chunk(slot, h):
         return rb.at[slot, pl.ds(h * (TOK // 2), TOK // 2)]
@@ -145,7 +200,7 @@
 
     go(ring(0, 0, 0))
     go(ring(1, 0, 0))
-    jump = go(remote(mine, wz_b.at[1, z], j_send, j_recv, at(y_=ys(4))))
+    jump = go(remote(mine, wz_b.at[z], j_send, j_recv, at(y_=ys(4))))
     go(ring(0, 0, 1))
     go(ring(1, 0, 1))
 
@@ -162,67 +217,77 @@
     r_s = jnp.where(r_i >= SLICE, 1, 0)
     r_f = r_i - r_s * SLICE
     r_b = tenth(r_f)
+    q_i = rows_of(SLICE)
+    q_b = tenth(q_i)
+    pick_near[...] = ones_at(q_b * PAD + q_i - q_b * ROWS, NZH * 8 * PAD)
     pick[...] = ones_at((r_b & 7) * COL + (r_s * NZH + (r_b >> 3)) * ROWS + r_f - r_b * ROWS, NX * 2 * COL)
 
-    higher(0, 1, 2)
     forward(1, 0)
-    higher(0, 3, 4)
+    higher(1, 2, 3, 4)
+    from_lower()
+    higher(5, 6, 7)
+    jump.wait_recv()
+    for k in range(1, NZ):
+        go(give(1, lax.rem(z + k, NZ)))
+    onward_lower()
     forward(1, 1)
-    higher(0, 5, 6, 7)
-    jump.wait_recv()
-
-    def spread(w):
-        def block(k, part=None):
-            ref = wcol.at[w, xs(k), core]
-            return ref if part is None else ref.at[pl.ds(*part)]
-
-        def over(i, k, src):
-            return go(remote(src, src, wx_send.at[w, i], wx_recv.at[w, i], at(x_=xs(k))))
-
-        def share(k):
-            shares.append(go(remote(block(k), block(k), ws_send.at[w, k % NX], ws_recv.at[w, k % NX], sibling)))
-
-        own, shares = [], []
-
-        def first():
-            gathered(w)
-            wcol[w, x, core] = jnp.dot(
-                pick_col, wz_b[w].reshape(NZ * PAD, COLS), preferred_element_type=F32).astype(BF16)
-            own.extend(over(i, k, block(0)) for i, k in enumerate((1, -1)))
-            share(0)
-
-        def second():
-            for i, (k, part) in enumerate(((1, (0, 48)), (-1, (48, 32)))):
-                own[i].wait_recv()
-                own.append(over(2 + i, k, block(-k, part)))
-                share(-k)
-
-        def third():
-            own[2].wait_recv()
-            own[3].wait_recv()
-            share(2)
-
-        def last():
-            for c in shares:
-                c.wait_recv()
-            wc[w] = jnp.dot(
-                pick[...], wcol[w].reshape(NX * 2 * COL, COLS), preferred_element_type=F32).astype(BF16)
-
-        return first, second, third, last
-
-    near, far = spread(0), spread(1)
-    near[0]()
+    shares = [near_share(0)]
+    onward_higher()
+    shares += [near_share(1), near_share(-1)]
     forward(2, 0)
-    lower(1)
-    higher(1, *range(1, NZ))
+
+    def column(k, part=None):
+        ref = wcol.at[xs(k), core]
+        return ref if part is None else ref.at[pl.ds(*part)]
+
+    def far_over(i, k, src):
+        return go(remote(src, src, wx_send.at[i], wx_recv.at[i], at(x_=xs(k))))
+
+    far_own, far_shares = [], []
+
+    def far_share(k):
+        far_shares.append(go(remote(column(k), column(k), ws_send.at[k % NX], ws_recv.at[k % NX], sibling)))
+
+    def far_first():
+        gathered()
+        wcol[x, core] = jnp.dot(
+            pick_col, wz_b[...].reshape(NZ * PAD, COLS), preferred_element_type=F32).astype(BF16)
+        far_own.extend(far_over(i, k, column(0)) for i, k in enumerate((1, -1)))
+        far_share(0)
+
+    def far_second():
+        for i, (k, part) in enumerate(((1, (0, 48)), (-1, (48, 32)))):
+            far_own[i].wait_recv()
+            far_own.append(far_over(2 + i, k, column(-k, part)))
+            far_share(-k)
+
+    def far_third():
+        far_own[2].wait_recv()
+        far_own[3].wait_recv()
+        far_share(2)
+
+    def far_last():
+        for c in far_shares:
+            c.wait_recv()
+        wc[1] = jnp.dot(
+            pick[...], wcol[...].reshape(NX * 2 * COL, COLS), preferred_element_type=F32).astype(BF16)
+
+    for b in range(NZ):
+        near_on(b, b % 2).wait_recv()
+    shares.append(near_share(2))
+    send_t = go(remote(tok_hbm.at[:, other], tb.at[zl], t_send.at[1], t_recv.at[1], partner))
     wp_part = pl.ds(pl.multiple_of(core * (SLICE // 2), SLICE // 2), SLICE // 2)
-    send_wp = go(remote(wp_hbm.at[wp_part], wpb.at[zl, wp_part], t_send.at[0], t_recv.at[0], partner))
-    send_t = go(remote(tok_hbm.at[:, other], tb.at[zl], t_send.at[1], t_recv.at[1], partner))
+    send_wp = go(remote(wp_hbm.at[wp_part], wpb.at[zl, wp_part], t_send.at[0], t_recv.at[0],
+                        at(z_=lax.rem(z + 2 * zl + NZ - 1, NZ))))
     forward(2, 1)
-    near[1]()
     forward(3, 0)
-    near[2]()
-    near[3]()
+    forward(3, 1)
+    for c in shares:
+        c.wait_recv()
+    for s in range(2):
+        rows = wg[s].reshape(NZH * 8 * PAD, COLS)
+        wc[0, pl.ds(s * SLICE, SLICE), :] = jnp.dot(
+            pick_near[...], rows, preferred_element_type=F32).astype(BF16)
 
     gsend = []
 
@@ -238,10 +303,10 @@
         send_g(2 * d - 1, d)
 
     gradient(1)
-    forward(3, 1)
     gradient(2)
+    far_first()
     gradient(3)
-    far[0]()
+    far_second()
     loads[2].wait()
     send_wp.wait_recv()
     share_wp = go(remote(wpb.at[1 - zl, wp_part], wpb.at[1 - zl, wp_part], t_send.at[2], t_recv.at[2], sibling))
@@ -265,7 +330,7 @@
     loads[3].wait()
     first = [scores(zl, pair) for pair in range(4)]
     gb[y] = dot_nt(rb[OWN], wc[0]).astype(BF16)
-    far[1]()
+    far_third()
     send_t.wait_recv()
     psend = []
     for pair in range(4):
@@ -283,17 +348,16 @@
     loads[5].wait()
     pos = tp * TOK + lax.broadcasted_iota(jnp.int32, (8, TOK), 1)
     start = jnp.int32(0)
-    shares = jnp.zeros((8, TOK), F32)
+    portion = jnp.zeros((8, TOK), F32)
     for k in range(8):
         n = lens[0, k]
         inside = (pos >= start) & (pos < start + n)
         frac = 1.0 / (8.0 * jnp.broadcast_to(n, (8, TOK)).astype(F32))
-        shares = shares + jnp.where(inside, frac, 0.0)
+        portion = portion + jnp.where(inside, frac, 0.0)
         start = start + n
-    base = -LOSS_MULTIPLIER * 2048.0 * shares
-
-    far[2]()
-    far[3]()
+    base = -LOSS_MULTIPLIER * 2048.0 * portion
+
+    far_last()
     gb[ys(4)] = dot_nt(rb[OWN], wc[1]).astype(BF16)
 
     for c in psend:
@@ -313,8 +377,7 @@
 
     for c in started:
         c.wait_send()
-    settle(0)
-    settle(1)
+    settle()
 
 
 def local(tokens, proximal_weight, current_weight, readout, advantage, lengths):
@@ -329,11 +392,13 @@
             vmem((8, TOK, COLS), BF16),
             vmem((2, SLICE, SEG), BF16),
             vmem((2, SLICE, COLS), BF16),
-            vmem((2, NZ, PAD, COLS), BF16),
-            vmem((2, NX, 2, COL, COLS), BF16),
+            vmem((2, NZH, NX, 2, PAD, COLS), BF16),
+            vmem((NZ, PAD, COLS), BF16),
+            vmem((NX, 2, COL, COLS), BF16),
             vmem((2, 2 * SLICE, COLS), BF16),
             vmem((2, SLICE, COLS), BF16),
             vmem((2 * SLICE, NX * 2 * COL), BF16),
+            vmem((SLICE, NZH * 8 * PAD), BF16),
             vmem((6, TOK, 2 * SLICE), BF16),
             vmem((8, TOK, 2 * SLICE), BF16),
             vmem((8, 8, TOK), F32),
@@ -342,7 +407,8 @@
             vmem((1, TOK), F32),
             pltpu.SMEM((1, 8), jnp.int32),
             dma((6,)), dma((2, 7)), dma((2, 7)), dma((2, 8)), dma((2, 8)),
-            dma((2, 4)), dma((2, 4)), dma((2, 4)), dma((2, 4)),
+            dma((4,)), dma((4,)), dma((4,)), dma((4,)),
+            dma((2, 8)), dma((2, 8)), dma((8,)), dma((8,)), dma((4,)), dma((4,)),
             dma((3,)), dma((3,)), dma((8,)), dma((8,)), dma((8,)), dma((8,)), dma, dma,
         ],
         compiler_params=pltpu.CompilerParams(

time: 67.4 us -> 66.5 us (0.987)
  the two profiles are of different devices: /device:TPU:1 before, /device:TPU:448 now
where the time goes in v4:
time: 66.5 us; the launch traced here: 66.3 us
  Pallas kernels  63.9 us (96%)
  local copies, waits for them, and re-layouts  2.46 us (4%)
    pallas_call x1, Pallas kernels, local(): pl.pallas_call(kernel, out_shape=jax.ShapeDtypeStruct((TOK, OUT), BF16),...  63.9 us
    unnamed x1, local copies, waits for them, and re-layouts  2.46 us

profile of v4, /device:TPU:448, one launch (start us, length us, event | category | flops | bytes accessed | tf_op | source)
XLA Modules:
  0.0 66.3 jit_solution(15421162997802357596)
XLA Ops:
  0.0 63.9 %shard_map.64 = bf16[128,5120]{1,0:T(8,128)(2,1)} custom-call(bf16[320,2048]{1,0:T(8,128)(2,1)} %bitcast.6, bf16[320,1024]{1,0:T(8,128)(2,1)} %wp_hbm.1, bf16[10,1024]{1,0:T(8,128)(2,1)} %wc_hbm.1, bf16[128,1024]{1,0:T(8,128)(2,1)} %bitcast.7, f32[1,128]{1,0:T(1,128)} %adv_hbm.1, s32[1,8]{1,0:T(1,128)} %len_hbm.1), custom_call_target="tpu_custom_call" | custom-call | flops 5000000000 | bytes 4000000 | tf_op jit(solution)/shard_map/pallas_call | solution.py:386
  63.9 2.5 %copy.8 = bf16[1,128,5120]{2,1,0:T(8,128)(2,1)} copy(bf16[1,128,5120]{2,1,0:T(8,128)(2,1)} %bitcast.5) | data formatting | bytes 2621440

commit v5 on v4

--- a/solution.py
+++ b/solution.py
@@ -222,8 +222,9 @@
     pick_near[...] = ones_at(q_b * PAD + q_i - q_b * ROWS, NZH * 8 * PAD)
     pick[...] = ones_at((r_b & 7) * COL + (r_s * NZH + (r_b >> 3)) * ROWS + r_f - r_b * ROWS, NX * 2 * COL)
 
+    higher(1, 2)
     forward(1, 0)
-    higher(1, 2, 3, 4)
+    higher(3, 4)
     from_lower()
     higher(5, 6, 7)
     jump.wait_recv()
@@ -282,6 +283,7 @@
     forward(2, 1)
     forward(3, 0)
     forward(3, 1)
+    far_first()
     for c in shares:
         c.wait_recv()
     for s in range(2):
@@ -304,7 +306,6 @@
 
     gradient(1)
     gradient(2)
-    far_first()
     gradient(3)
     far_second()
     loads[2].wait()
@@ -368,6 +369,10 @@
     eye = ones_at(rows_of(TOK), TOK).astype(F32)
     scale = jnp.sum(jnp.where(eye > 0.0, coef, 0.0), axis=1, keepdims=True)
 
+    settle()
+    for c in started:
+        if all(c is not g for g in gsend):
+            c.wait_send()
     for c in gsend:
         c.wait_recv()
     for i in range(NY):
@@ -375,9 +380,8 @@
         for s in range(2):
             out_ref[:, (s * NY + i) * SLICE:(s * NY + i + 1) * SLICE] = g[:, s * SLICE:(s + 1) * SLICE].astype(BF16)
 
-    for c in started:
+    for c in gsend:
         c.wait_send()
-    settle()
 
 
 def local(tokens, proximal_weight, current_weight, readout, advantage, lengths):

time: 66.5 us -> 66.5 us (level)
  no operation moved by 1% of the time
where the time goes in v5:
time: 66.5 us; the launch traced here: 66.3 us
  Pallas kernels  63.8 us (96%)
  local copies, waits for them, and re-layouts  2.46 us (4%)
    pallas_call x1, Pallas kernels, local(): pl.pallas_call(kernel, out_shape=jax.ShapeDtypeStruct((TOK, OUT), BF16),...  63.8 us
    unnamed x1, local copies, waits for them, and re-layouts  2.46 us

profile of v5, /device:TPU:448, one launch (start us, length us, event | category | flops | bytes accessed | tf_op | source)
XLA Modules:
  0.0 66.3 jit_solution(16443279493725005489)
XLA Ops:
  0.0 63.8 %shard_map.64 = bf16[128,5120]{1,0:T(8,128)(2,1)} custom-call(bf16[320,2048]{1,0:T(8,128)(2,1)} %bitcast.6, bf16[320,1024]{1,0:T(8,128)(2,1)} %wp_hbm.1, bf16[10,1024]{1,0:T(8,128)(2,1)} %wc_hbm.1, bf16[128,1024]{1,0:T(8,128)(2,1)} %bitcast.7, f32[1,128]{1,0:T(1,128)} %adv_hbm.1, s32[1,8]{1,0:T(1,128)} %len_hbm.1), custom_call_target="tpu_custom_call" | custom-call | flops 5000000000 | bytes 4000000 | tf_op jit(solution)/shard_map/pallas_call | solution.py:390
  63.9 2.5 %copy.8 = bf16[1,128,5120]{2,1,0:T(8,128)(2,1)} copy(bf16[1,128,5120]{2,1,0:T(8,128)(2,1)} %bitcast.5) | data formatting | bytes 2621440

commit v6 on v5

--- a/solution.py
+++ b/solution.py
@@ -36,7 +36,7 @@
 
 
 def kernel(tok_hbm, wp_hbm, wc_hbm, r_hbm, adv_hbm, len_hbm, out_ref,
-           rb, tb, wpb, wg, wz_b, wcol, wc, dw, pick, pick_near, gs, gb, ps, sb, wc_own, adv, lens,
+           rb, tb, wpb, wg, wz_b, wcol, wc, dw, pick, pick_near, gs, gb, ps, sb, adv, lens,
            loc, r_send, r_recv, wz_send, wz_recv, wx_send, wx_recv, ws_send, ws_recv, nx_send, nx_recv, ny_send, ny_recv, ns_send, ns_recv,
            t_send, t_recv, g_send, g_recv, p_send, p_recv, j_send, j_recv):
     tp, dp = lax.axis_index("tp"), lax.axis_index("dp")
@@ -84,15 +84,13 @@
 
     half = pl.ds(pl.multiple_of(zl * SEG, SEG), SEG)
     other = pl.ds(pl.multiple_of((1 - zl) * SEG, SEG), SEG)
+    mine = wg.at[zl, zh, x, core]
     loads = [pltpu.make_async_copy(src, dst, loc.at[i]) for i, (src, dst) in enumerate((
-        (wc_hbm, wc_own), (r_hbm, rb.at[OWN]), (wp_hbm, wpb.at[zl]), (tok_hbm.at[:, half], tb.at[zl]),
+        (wc_hbm, mine), (r_hbm, rb.at[OWN]), (wp_hbm, wpb.at[zl]), (tok_hbm.at[:, half], tb.at[zl]),
         (adv_hbm, adv), (len_hbm, lens)))]
     for load in loads:
         load.start()
-    mine = wg.at[zl, zh, x, core]
-    mine[...] = jnp.zeros((PAD, COLS), BF16)
     loads[0].wait()
-    mine[pl.ds(0, ROWS), :] = wc_own[...]
     loads[1].wait()
     pl.semaphore_wait(barrier, len(peers) + z)
 
@@ -407,7 +405,6 @@
             vmem((8, TOK, 2 * SLICE), BF16),
             vmem((8, 8, TOK), F32),
             vmem((8, 8, TOK), F32),
-            vmem((ROWS, COLS), BF16),
             vmem((1, TOK), F32),
             pltpu.SMEM((1, 8), jnp.int32),
             dma((6,)), dma((2, 7)), dma((2, 7)), dma((2, 8)), dma((2, 8)),
@@ -418,7 +415,8 @@
         compiler_params=pltpu.CompilerParams(
             collective_id=0, has_side_effects=True, vmem_limit_bytes=VMEM_LIMIT),
         cost_estimate=pl.CostEstimate(flops=5 * 10**9, bytes_accessed=4 * 10**6, transcendentals=1024),
-    )(jnp.swapaxes(tokens[0], 0, 1), proximal_weight, current_weight, readout[0], advantage, lengths)
+    )(jnp.swapaxes(tokens[0], 0, 1), proximal_weight, jnp.pad(current_weight, ((0, PAD - ROWS), (0, 0))),
+      readout[0], advantage, lengths)
     return out[None]
 
 

time: 66.5 us -> 67.9 us (1.021)
  local copies, waits for them, and re-layouts: 2.46 us -> 3.84 us
    pad x0 -> x1, local copies, waits for them, and re-layouts: none -> 1.38 us  [local(): jnp.pad(current_weight, ((0, PAD - ROWS), (0, 0)))]
where the time goes in v6:
time: 67.9 us; the launch traced here: 67.7 us
  Pallas kernels  63.8 us (94%)
  local copies, waits for them, and re-layouts  3.84 us (6%)
    pallas_call x1, Pallas kernels, local(): pl.pallas_call(kernel, out_shape=jax.ShapeDtypeStruct((TOK, OUT), BF16),...  63.8 us
    unnamed x1, local copies, waits for them, and re-layouts  2.46 us
    pad x1, local copies, waits for them, and re-layouts, local(): jnp.pad(current_weight, ((0, PAD - ROWS), (0, 0)))  1.38 us

profile of v6, /device:TPU:448, one launch (start us, length us, event | category | flops | bytes accessed | tf_op | source)
XLA Modules:
  0.0 67.7 jit_solution(16738056852650547805)
XLA Ops:
  0.0 1.4 %pad.4.wc_hbm = bf16[16,1024]{1,0:T(8,128)(2,1)} pad(bf16[10,1024]{1,0:T(8,128)(2,1)} %param.8, bf16[]{:T(256)} %constant.2.clone.1), padding=0_6x0_0 | pad | bytes 53250 | tf_op jit(solution)/shard_map/jit(_pad)/pad | solution.py:418
  1.4 63.8 %shard_map.64 = bf16[128,5120]{1,0:T(8,128)(2,1)} custom-call(bf16[320,2048]{1,0:T(8,128)(2,1)} %bitcast.6, bf16[320,1024]{1,0:T(8,128)(2,1)} %wp_hbm.1, bf16[16,1024]{1,0:T(8,128)(2,1)} %pad.4.wc_hbm, bf16[128,1024]{1,0:T(8,128)(2,1)} %bitcast.7, f32[1,128]{1,0:T(1,128)} %adv_hbm.1, s32[1,8]{1,0:T(1,128)} %len_hbm.1), custom_call_target="tpu_custom_call" | custom-call | flops 5000000000 | bytes 4000000 | tf_op jit(solution)/shard_map/pallas_call | solution.py:388
  65.2 2.5 %copy.8 = bf16[1,128,5120]{2,1,0:T(8,128)(2,1)} copy(bf16[1,128,5120]{2,1,0:T(8,128)(2,1)} %bitcast.5) | data formatting | bytes 2621440
